TPU v7x, 256 devices: a whole 4x4x8 slice. The times are simulated.
256 devices in a mesh: section: 32 (over y, z), dp: 2 (over x_lo), tensor: 4 (over x_hi, core).
Axes of the slice: x: 4 (x_hi: 2, x_lo: 2; x = x_hi * 2 + x_lo), y: 4, z: 8, core: 2. Of those that a mesh axis runs over, the one named last changes fastest.
Arguments:
- inputs: bfloat16 [32, 2, 256, 3584], P('section', 'dp', None, 'tensor'), may hold values from -8 to 8
- qkv_weight: bfloat16 [32, 3, 3584, 3584], P('section', None, 'dp', 'tensor')
- norm_gain: bfloat16 [32, 3584], P('section'), may hold values from 0.25 to 1.75
- preempted: int32 [32], P('section'), may hold values 0 or 1
Outputs:
- outputs: bfloat16 [32, 2, 256, 3584], P('section', 'dp', None, 'tensor')
All inputs are finite; a program needn't handle non-finite values. No bound on the sum of `preempted` on one device may be relied on, other than what follows from the above.
Results may differ from a plain program's by a relative error of at most 0.008.
Values may be sent and summed in bfloat16 or wider, within the bound.
A program may use at most 64 MiB of HBM per device.

v0:
```python
import jax
import jax.numpy as jnp
from jax import lax
from jax.sharding import PartitionSpec as P

HD = 128


def from_behind(array, axis, by):
    size = lax.axis_size(axis)
    pairs = [(i, i + by) for i in range(size) if 0 <= i + by < size]
    return lax.ppermute(array, axis, pairs)


def project(normed, weight):
    all_rows = lax.all_to_all(normed, "dp", split_axis=1, concat_axis=0, tiled=True)
    return lax.psum_scatter(
        jnp.einsum("rd,kde->rke", all_rows, weight, preferred_element_type=jnp.float32),
        "dp",
        scatter_dimension=0,
        tiled=True,
    )


def gather_rows(hidden_in):
    return lax.all_gather(hidden_in, "tensor", axis=2, tiled=True)


def attend(hidden_in, gathered, weight, gain_row):
    seq_count, length, local_width = hidden_in.shape
    float_acts = gathered.astype(jnp.float32)
    inverse_rms = lax.rsqrt(jnp.mean(float_acts * float_acts, axis=-1, keepdims=True) + 1e-05)
    normed = (float_acts * inverse_rms * gain_row).astype(jnp.bfloat16)
    flat_rows = normed.reshape(seq_count * length, gathered.shape[2])
    projected = project(flat_rows, weight).astype(jnp.bfloat16)
    head_size = HD
    local_heads = local_width // head_size
    head_shape = (seq_count, length, local_heads, head_size)
    queries = projected[:, 0].reshape(head_shape)
    key_rows = projected[:, 1].reshape(head_shape)
    values = projected[:, 2].reshape(head_shape)
    scores = jnp.einsum(
        "sqhd,skhd->shqk", queries, key_rows, preferred_element_type=jnp.float32
    ) / jnp.sqrt(jnp.float32(head_size))
    causal = jnp.arange(length)[:, None] >= jnp.arange(length)[None, :]
    scores = jnp.where(causal, scores, jnp.float32(-1e30))
    probability = jax.nn.softmax(scores, axis=-1).astype(jnp.bfloat16)
    mixture = jnp.einsum("shqk,skhd->sqhd", probability, values, preferred_element_type=jnp.float32)
    return (hidden_in.astype(jnp.float32) + mixture.reshape(seq_count, length, local_width)).astype(
        jnp.bfloat16
    )


def local(inputs, qkv_weight, norm_gain, preempted):
    hidden_in = inputs[0]
    weight = qkv_weight[0]
    gain_row = norm_gain[0]
    own_out = attend(hidden_in, gather_rows(hidden_in), weight, gain_row)
    before = from_behind(own_out, "section", 1)
    recovered = attend(before, gather_rows(before), weight, gain_row)
    result = jnp.where(preempted[0] == 1, recovered, own_out)
    return result[None]


def solution(mesh):
    placed = (
        P("section", "dp", None, "tensor"),
        P("section", None, "dp", "tensor"),
        P("section", None),
        P("section"),
    )
    return jax.shard_map(
        local,
        mesh=mesh,
        in_specs=placed,
        out_specs=P("section", "dp", None, "tensor"),
        check_vma=False,
    )
```

profile of v0, /device:TPU:24, one launch (start us, length us, event | category | flops | bytes accessed | tf_op | source)
XLA Modules:
  0.0 342.0 jit_solution(17617839566345494523)
XLA Ops:
  6.5 0.7 all-gather.6.cloned.1.call-update
  7.3 0.0 reduce-scatter.3.cloned.1.call-start
  7.3 0.8 convert_reduce_fusion
  8.1 31.5 %all-gather.6.cloned.1.call-done = bf16[1,1,256,3584]{3,2,1,0:T(8,128)(2,1)} async-done(((bf16[1,1,256,896]{3,2,1,0:T(8,128)(2,1)}), bf16[1,1,256,3584]{3,2,1,0:T(8,128)(2,1)}) %all-gather.6.cloned.1.call-update) | async-done | bytes 1835024 | tf_op jit(solution)/shard_map/all_gather | solution.py:26
  39.6 2.1 fusion.9
  41.7 1.8 fusion.11
  43.5 4.0 %all_to_all.28 = bf16[256,2,1792]{2,1,0:T(2,128)(2,1)S(1)} reshape(bf16[1,256,3584]{2,1,0:T(8,128)(2,1)} %fusion.11) | data formatting | bytes 3670016 | tf_op jit(solution)/shard_map/all_to_all | solution.py:16
  47.5 0.2 copy.17
  47.7 25.2 %all_to_all.38 = bf16[256,2,1792]{2,0,1:T(8,128)(2,1)S(1)} all-to-all(bf16[256,2,1792]{2,0,1:T(8,128)(2,1)S(1)} %copy.17), channel_id=1, replica_groups=mesh['section'=32,'dp'=2,'tensor'=4] {'dp'}, dimensions={1} | all-to-all | bytes 3670016 | tf_op jit(solution)/shard_map/all_to_all | solution.py:16
  72.9 11.0 %fusion.4 = f32[512,3,896]{2,0,1:T(8,128)} fusion(bf16[512,1792,1]{1,0,2:T(8,128)(2,1)S(1)} %bitcast.49, bf16[1,3,1792,896]{3,2,1,0:T(8,128)(2,1)} %param.5), kind=kOutput, calls=%fused_computation.4 | convolution fusion | flops 4932501504 | bytes 16973824 | tf_op jit(solution)/shard_map/rd,kde->rke/dot_general | solution.py:18
  83.9 0.0 reduce-scatter.3.cloned.1.call-update
  84.0 0.0 all-gather.4.cloned.1.call-start
  84.0 72.9 %reduce-scatter.3.cloned.1.call-done = f32[256,3,896]{2,0,1:T(8,128)} async-done(((f32[512,3,896]{2,0,1:T(8,128)}), f32[256,3,896]{2,0,1:T(8,128)}) %reduce-scatter.3.cloned.1.call-update) | async-done | bytes 2752528 | tf_op jit(solution)/shard_map/reduce_scatter | solution.py:17
  156.9 1.9 convert_element_type.70
  158.8 0.1 fusion.34
  158.9 0.2 copy.20
  159.2 0.2 copy.19
  159.4 0.2 copy.18
  159.6 2.0 fusion.35
  161.6 1.8 fusion.19
  163.4 0.3 copy.24
  163.7 0.7 copy-done.2
  164.4 0.1 fusion.14
  164.5 3.5 %collective-permute-start = (bf16[1,256,896]{2,1,0:T(8,128)(2,1)S(1)}, bf16[1,256,896]{2,1,0:T(8,128)(2,1)S(1)}, u32[]{:S(2)}, u32[]{:S(2)}) collective-permute-start(bf16[1,256,896]{2,1,0:T(8,128)(2,1)S(1)} %fusion.14), channel_id=1, source_target_pairs={{0,8},{8,16},{16,24},{24,32},{32,40},{40,48},{48,56},{56,64},{64,7... | collective-permute-start | bytes 1376264 | tf_op jit(solution)/shard_map/ppermute | solution.py:12
  168.0 12.8 %collective-permute-done = bf16[1,256,896]{2,1,0:T(8,128)(2,1)S(1)} collective-permute-done((bf16[1,256,896]{2,1,0:T(8,128)(2,1)S(1)}, bf16[1,256,896]{2,1,0:T(8,128)(2,1)S(1)}, u32[]{:S(2)}, u32[]{:S(2)}) %collective-permute-start) | collective-permute-done | bytes 458784 | tf_op jit(solution)/shard_map/ppermute | solution.py:12
  180.8 0.8 copy-done.3
  181.6 0.0 all-gather.4.cloned.1.call-update
  181.6 0.0 reduce-scatter.5.cloned.1.call-start
  181.6 27.9 %all-gather.4.cloned.1.call-done = bf16[1,256,3584]{2,1,0:T(8,128)(2,1)} async-done(((bf16[1,256,896]{2,1,0:T(8,128)(2,1)}), bf16[1,256,3584]{2,1,0:T(8,128)(2,1)}) %all-gather.4.cloned.1.call-update) | async-done | bytes 1835024 | tf_op jit(solution)/shard_map/all_gather | solution.py:26
  209.6 2.1 fusion.6
  211.6 1.8 fusion.8
  213.4 4.0 %all_to_all.32 = bf16[256,2,1792]{2,1,0:T(2,128)(2,1)S(1)} reshape(bf16[1,256,3584]{2,1,0:T(8,128)(2,1)} %fusion.8) | data formatting | bytes 3670016 | tf_op jit(solution)/shard_map/all_to_all | solution.py:16
  217.5 0.2 copy.25
  217.7 25.2 %all_to_all.39 = bf16[256,2,1792]{2,0,1:T(8,128)(2,1)S(1)} all-to-all(bf16[256,2,1792]{2,0,1:T(8,128)(2,1)S(1)} %copy.25), channel_id=1, replica_groups=mesh['section'=32,'dp'=2,'tensor'=4] {'dp'}, dimensions={1} | all-to-all | bytes 3670016 | tf_op jit(solution)/shard_map/all_to_all | solution.py:16
  242.9 11.0 %fusion.2 = f32[512,3,896]{2,0,1:T(8,128)} fusion(bf16[512,1792,1]{1,0,2:T(8,128)(2,1)S(1)} %bitcast.50, bf16[1,3,1792,896]{3,2,1,0:T(8,128)(2,1)} %param.5), kind=kOutput, calls=%fused_computation.2 | convolution fusion | flops 4932501504 | bytes 16973824 | tf_op jit(solution)/shard_map/rd,kde->rke/dot_general | solution.py:18
  253.9 0.0 reduce-scatter.5.cloned.1.call-update
  254.5 72.5 %reduce-scatter.5.cloned.1.call-done = f32[256,3,896]{2,0,1:T(8,128)} async-done(((f32[512,3,896]{2,0,1:T(8,128)}), f32[256,3,896]{2,0,1:T(8,128)}) %reduce-scatter.5.cloned.1.call-update) | async-done | bytes 2752528 | tf_op jit(solution)/shard_map/reduce_scatter | solution.py:17
  327.0 1.9 convert_element_type.76
  329.0 0.1 fusion.33
  329.1 0.2 copy.27
  329.3 0.2 copy.28
  329.5 0.2 copy.26
  329.7 2.0 fusion.36
  331.8 1.8 fusion.20
  333.6 0.0 copy-start.4
  333.6 0.3 copy.32
  333.9 0.7 copy-done.4
  334.6 0.9 fusion.24
  (10 shorter events, 0.1 us)
Async XLA Ops:
  6.5 33.1 %all-gather.6.cloned.1.call-start = ((), (), s32[]{:S(2)}) async-start(), calls=%async_computation.7 | async-start | bytes 2293760 | tf_op jit(solution)/shard_map/all_gather | solution.py:26
  7.3 149.6 %reduce-scatter.3.cloned.1.call-start = ((), (), s32[]{:S(2)}) async-start(), calls=%async_computation.4 | async-start | bytes 8257536 | tf_op jit(solution)/shard_map/reduce_scatter | solution.py:17
  39.6 2.1 copy-start
  84.0 125.6 %all-gather.4.cloned.1.call-start = ((), (), s32[]{:S(2)}) async-start(), calls=%async_computation.5 | async-start | bytes 2293760 | tf_op jit(solution)/shard_map/all_gather | solution.py:26
  163.4 1.0 copy-start.2
  164.5 16.3 %collective-permute-start = (bf16[1,256,896]{2,1,0:T(8,128)(2,1)S(1)}, bf16[1,256,896]{2,1,0:T(8,128)(2,1)S(1)}, u32[]{:S(2)}, u32[]{:S(2)}) collective-permute-start(bf16[1,256,896]{2,1,0:T(8,128)(2,1)S(1)} %fusion.14), channel_id=1, source_target_pairs={{0,8},{8,16},{16,24},{24,32},{32,40},{40,48},{48,56},{56,64},{64,7... | collective-permute-start | bytes 1376264 | tf_op jit(solution)/shard_map/ppermute | solution.py:12
  180.8 0.8 copy-start.3
  181.6 145.4 %reduce-scatter.5.cloned.1.call-start = ((), (), s32[]{:S(2)}) async-start(), calls=%async_computation.6 | async-start | bytes 8257536 | tf_op jit(solution)/shard_map/reduce_scatter | solution.py:17
  209.6 2.1 copy-start.1
  333.6 1.0 copy-start.4
Sparse Core Ops, SparseCore 0:
  9.2 30.3 all-gather.5
  84.1 72.7 reduce-scatter.2
  181.7 27.7 all-gather.3
  254.0 72.9 reduce-scatter.4
where the time goes:
time: 344 us; the launch traced here: 342 us
  waiting for transfers between devices  218 us (63%)
  blocking collectives  50.5 us (15%)
  matrix products  29.6 us (9%)
  between operations  13.9 us (4%)
  other arithmetic  13.3 us (4%)
  local copies, waits for them, and re-layouts  12.7 us (4%)
  starting transfers between devices  3.59 us (1%)
    reduce_scatter x2, waiting for transfers between devices, project(): lax.psum_scatter(jnp.einsum('rd,kde->rke', all_rows, weight, preferred_el...  145 us
    all_gather x2, waiting for transfers between devices, gather_rows(): return lax.all_gather(hidden_in, 'tensor', axis=2, tiled=True)  59.5 us
    all_to_all x2, blocking collectives, project(): lax.all_to_all(normed, 'dp', split_axis=1, concat_axis=0, tiled=True)  50.5 us
    dot_general x2, matrix products, project(): jnp.einsum('rd,kde->rke', all_rows, weight, preferred_element_type=jnp.fl...  22 us
    ppermute x1, waiting for transfers between devices, from_behind(): return lax.ppermute(array, axis, pairs)  12.8 us
    all_to_all x4, local copies, waits for them, and re-layouts, project(): lax.all_to_all(normed, 'dp', split_axis=1, concat_axis=0, tiled=True)  8.45 us
  transfers between devices with their start and end apart: 5, of which 5 were waited for; matrix products, arithmetic and copies ran while one was open for 0% of the time, Pallas kernels for 0%

commit v1 on v0

v1 whole, which is shorter than its diff:
```python
import functools
import math

import jax
import jax.numpy as jnp
from jax import lax
from jax.experimental import pallas as pl
from jax.experimental.pallas import tpu as pltpu
from jax.sharding import PartitionSpec as P

HD = 128
LAG = 3
MESH = pl.DeviceIdType.MESH


def kernel(
    sections,
    heads,
    a_hbm,
    w_hbm,
    gain_hbm,
    pre_ref,
    out_hbm,
    w,
    feats,
    psend,
    precv,
    a_own,
    x_prev,
    own,
    final,
    gain,
    squares,
    scale,
    note,
    heard,
    w_sem,
    in_sem,
    out_sem,
    q_send,
    q_recv,
    p_send,
    p_recv,
    s_send,
    s_recv,
    part_send,
    part_recv,
    hop_send,
    hop_recv,
    note_send,
    note_recv,
):
    s, d, t = lax.axis_index("section"), lax.axis_index("dp"), lax.axis_index("tensor")
    high, core = t // 2, t % 2
    rows, width = a_own.shape
    features = 4 * width

    partner = (s, 1 - d, t)
    other = (s, 1 - d, (1 - high) * 2 + core)
    sibling = (s, d, high * 2 + 1 - core)
    opposite = (s, d, (1 - high) * 2 + core)
    after = (lax.rem(s + 1, sections), d, t)
    before = (lax.rem(s + sections - 1, sections), d, t)

    straight = high == d
    mine = jnp.where(straight, 1, 2)
    to_other = jnp.where(straight, 2, 0)
    to_partner = jnp.where(straight, 1, 0)
    from_partner = jnp.where(straight, 0, 1)

    def columns(c, h):
        return pl.ds(pl.multiple_of(c * width + h * HD, HD), HD)

    def piece(layer, slot, c, h):
        return feats.at[layer, slot, :, columns(c, h)]

    def remote(src, dst, send, recv, device):
        return pltpu.make_async_remote_copy(
            src_ref=src, dst_ref=dst, send_sem=send, recv_sem=recv, device_id=device, device_id_type=MESH
        )

    def other_copy(layer, h):
        return remote(
            piece(layer, mine, core, h), piece(layer, to_other, core, h),
            q_send.at[layer, h], q_recv.at[layer, h], other,
        )

    def other_arrival(layer, h):
        there = piece(layer, to_other, core, h)
        return remote(there, there, q_send.at[layer, h], q_recv.at[layer, h], other)

    def partner_copy(layer, h):
        return remote(
            piece(layer, 2, core, h), piece(layer, to_partner, core, h),
            p_send.at[layer, h], p_recv.at[layer, h], partner,
        )

    def partner_arrival(layer, h):
        there = piece(layer, from_partner, core, h)
        return remote(there, there, p_send.at[layer, h], p_recv.at[layer, h], partner)

    def sibling_copy(layer, slot, h):
        here = piece(layer, slot, core, h)
        return remote(here, here, s_send.at[layer, slot, h], s_recv.at[layer, slot, h], sibling)

    def sibling_arrival(layer, slot, h):
        there = piece(layer, slot, 1 - core, h)
        return remote(there, there, s_send.at[layer, slot, h], s_recv.at[layer, slot, h], sibling)

    def part_copy(layer, g):
        return remote(
            psend.at[layer, g], precv.at[layer, g], part_send.at[layer, g], part_recv.at[layer, g], partner
        )

    def hop_copy(h):
        here = pl.ds(pl.multiple_of(h * HD, HD), HD)
        return remote(own.at[:, here], x_prev.at[:, here], hop_send.at[h], hop_recv.at[h], after)

    def note_copy(layer, i):
        return remote(
            note.at[layer, i], heard.at[layer, i], note_send.at[layer, i], note_recv.at[layer, i],
            (sibling, opposite)[i],
        )

    def w_copy(g, j):
        return pltpu.make_async_copy(
            w_hbm.at[j, :, pl.ds(pl.multiple_of(g * HD, HD), HD)],
            w.at[g, :, pl.ds(j * HD, HD)],
            w_sem.at[g, j],
        )

    def out_copy(h):
        here = pl.ds(pl.multiple_of(h * HD, HD), HD)
        return pltpu.make_async_copy(final.at[:, here], out_hbm.at[:, here], out_sem.at[h])

    a_copy = pltpu.make_async_copy(a_hbm, a_own, in_sem.at[0])
    gain_copy = pltpu.make_async_copy(gain_hbm, gain, in_sem.at[1])
    a_copy.start()
    gain_copy.start()

    @pl.loop(0, heads)
    def _(g):
        for j in range(3):
            w_copy(g, j).start()

    barrier = pltpu.get_barrier_semaphore()
    for device in (partner, other, sibling, opposite, before):
        pl.semaphore_signal(barrier, inc=1, device_id=device, device_id_type=MESH)
    pl.semaphore_wait(barrier, 5)

    a_copy.wait()
    gain_copy.wait()

    def layer_input(layer, h):
        here = pl.ds(pl.multiple_of(h * HD, HD), HD)
        if layer == 0:
            return a_own[:, here].astype(jnp.float32)
        return jnp.where(s == 0, 0.0, x_prev[:, here].astype(jnp.float32))

    def send_piece(layer, h):
        if layer == 1:
            hop_copy(h).wait_recv()
        x = layer_input(layer, h)
        squares[layer] += x * x
        row = gain[0:1, pl.ds(pl.multiple_of(t * width + h * HD, HD), HD)].astype(jnp.float32)
        feats[layer, mine, :, columns(core, h)] = (x * row).astype(jnp.bfloat16)
        other_copy(layer, h).start()

        @pl.when(straight)
        def _():
            sibling_copy(layer, 1, h).start()

        @pl.when(jnp.logical_not(straight))
        def _():
            partner_copy(layer, h).start()

    def pass_on(layer, h):
        other_arrival(layer, h).wait_recv()

        @pl.when(straight)
        def _():
            partner_copy(layer, h).start()
            partner_arrival(layer, h).wait_recv()

        sibling_copy(layer, 0, h).start()

    def late_pass_on(layer, h):
        partner_arrival(layer, h).wait_recv()
        sibling_copy(layer, 1, h).start()

    def tell_squares(layer):
        sums = jnp.sum(squares[layer], axis=1, keepdims=True)
        note[layer, 0] = jnp.broadcast_to(sums, (rows, HD)).T[0:8, :]
        note_copy(layer, 0).start()

    def tell_pair(layer):
        note_copy(layer, 0).wait_recv()
        note[layer, 1] = note[layer, 0] + heard[layer, 0]
        note_copy(layer, 1).start()

    def take_squares(layer):
        note_copy(layer, 1).wait_recv()
        total = note[layer, 1] + heard[layer, 1]
        inverse = lax.rsqrt(total * (1.0 / features) + 1e-05)
        scale[layer] = jnp.broadcast_to(inverse[0:1, :], (HD, rows)).T

    def send_parts(layer):
        @pl.loop(0, heads)
        def _(h):
            sibling_arrival(layer, 0, h).wait_recv()

        @pl.loop(0, heads)
        def _(g):
            if layer == 0:
                for j in range(3):
                    w_copy(g, j).wait()
            part = jnp.dot(feats[layer, 0], w[g], preferred_element_type=jnp.float32)
            psend[layer, g] = part.astype(jnp.bfloat16)
            part_copy(layer, g).start()

    def late_pieces(layer):
        @pl.when(jnp.logical_not(straight))
        def _():
            @pl.loop(0, heads)
            def _(h):
                late_pass_on(layer, h)

        @pl.loop(0, heads)
        def _(h):
            sibling_arrival(layer, 1, h).wait_recv()

    def attend(layer, g):
        part = jnp.dot(feats[layer, 1], w[g], preferred_element_type=jnp.float32)
        part_copy(layer, g).wait_recv()
        part = part + precv[layer, g].astype(jnp.float32)
        inverse = scale[layer]
        query = (part[:, 0:HD] * inverse).astype(jnp.bfloat16)
        key = (part[:, HD : 2 * HD] * inverse).astype(jnp.bfloat16)
        value = (part[:, 2 * HD :] * inverse).astype(jnp.bfloat16)
        scores = lax.dot_general(
            query, key, (((1,), (1,)), ((), ())), preferred_element_type=jnp.float32
        ) * (1.0 / math.sqrt(HD))
        causal = lax.broadcasted_iota(jnp.int32, (rows, rows), 0) >= lax.broadcasted_iota(
            jnp.int32, (rows, rows), 1
        )
        scores = jnp.where(causal, scores, jnp.float32(-1e30))
        powers = jnp.exp(scores - jnp.max(scores, axis=1, keepdims=True))
        chance = (powers * (1.0 / jnp.sum(powers, axis=1, keepdims=True))).astype(jnp.bfloat16)
        mixture = jnp.dot(chance, value, preferred_element_type=jnp.float32)
        return (layer_input(layer, g) + mixture).astype(jnp.bfloat16)

    squares[...] = jnp.zeros_like(squares)

    @pl.loop(0, heads)
    def _(h):
        send_piece(0, h)

    tell_squares(0)

    @pl.loop(0, heads)
    def _(h):
        pass_on(0, h)

    tell_pair(0)
    send_parts(0)
    late_pieces(0)
    take_squares(0)

    @pl.loop(0, heads)
    def _(g):
        here = pl.ds(pl.multiple_of(g * HD, HD), HD)
        own[:, here] = attend(0, g)
        hop_copy(g).start()

        @pl.when(g >= LAG)
        def _():
            send_piece(1, g - LAG)

    @pl.loop(heads - LAG, heads)
    def _(h):
        pass_on(1, h - (heads - LAG))
        send_piece(1, h)

    tell_squares(1)

    @pl.loop(LAG, heads)
    def _(h):
        pass_on(1, h)

    tell_pair(1)
    send_parts(1)
    late_pieces(1)
    take_squares(1)
    take = pre_ref[0] == 1

    @pl.loop(0, heads)
    def _(g):
        here = pl.ds(pl.multiple_of(g * HD, HD), HD)
        shadow = attend(1, g)
        final[:, here] = jnp.where(take, shadow, own[:, here])
        out_copy(g).start()

    @pl.loop(0, heads)
    def _(h):
        for layer in range(2):
            other_copy(layer, h).wait_send()
            partner_copy(layer, h).wait_send()
            sibling_copy(layer, 0, h).wait_send()
            sibling_copy(layer, 1, h).wait_send()
            part_copy(layer, h).wait_send()
        hop_copy(h).wait_send()
        out_copy(h).wait()

    for layer in range(2):
        for i in range(2):
            note_copy(layer, i).wait_send()


def local(sections, inputs, qkv_weight, norm_gain, preempted):
    rows, width = inputs.shape[2:]
    heads = width // HD
    depth = qkv_weight.shape[2]
    bf16, f32 = jnp.bfloat16, jnp.float32
    dma = pltpu.SemaphoreType.DMA
    any_space = pl.BlockSpec(memory_space=pl.ANY)
    result = pl.pallas_call(
        functools.partial(kernel, sections, heads),
        out_shape=jax.ShapeDtypeStruct((rows, width), bf16),
        in_specs=[any_space, any_space, any_space, pl.BlockSpec(memory_space=pltpu.SMEM)],
        out_specs=any_space,
        scratch_shapes=[
            pltpu.VMEM((heads, depth, 3 * HD), bf16),
            pltpu.VMEM((2, 3, rows, depth), bf16),
            pltpu.VMEM((2, heads, rows, 3 * HD), bf16),
            pltpu.VMEM((2, heads, rows, 3 * HD), bf16),
            pltpu.VMEM((rows, width), bf16),
            pltpu.VMEM((rows, width), bf16),
            pltpu.VMEM((rows, width), bf16),
            pltpu.VMEM((rows, width), bf16),
            pltpu.VMEM((1, 4 * width), bf16),
            pltpu.VMEM((2, rows, HD), f32),
            pltpu.VMEM((2, rows, HD), f32),
            pltpu.VMEM((2, 2, 8, rows), f32),
            pltpu.VMEM((2, 2, 8, rows), f32),
            dma((heads, 3)),
            dma((2,)),
            dma((heads,)),
            dma((2, heads)),
            dma((2, heads)),
            dma((2, heads)),
            dma((2, heads)),
            dma((2, 2, heads)),
            dma((2, 2, heads)),
            dma((2, heads)),
            dma((2, heads)),
            dma((heads,)),
            dma((heads,)),
            dma((2, 2)),
            dma((2, 2)),
        ],
        compiler_params=pltpu.CompilerParams(
            collective_id=0, has_side_effects=True, vmem_limit_bytes=48 * 2**20
        ),
        cost_estimate=pl.CostEstimate(
            flops=8 * rows * depth * 3 * width, bytes_accessed=qkv_weight.size * 2, transcendentals=0
        ),
        name="relay",
    )(inputs[0, 0], qkv_weight[0], norm_gain, preempted)
    return result[None, None]


def solution(mesh):
    placed = (
        P("section", "dp", None, "tensor"),
        P("section", None, "dp", "tensor"),
        P("section", None),
        P("section"),
    )
    return jax.shard_map(
        functools.partial(local, mesh.shape["section"]),
        mesh=mesh,
        in_specs=placed,
        out_specs=P("section", "dp", None, "tensor"),
        check_vma=False,
    )
```

time: 344 us -> 104 us (0.30)
  the two profiles are of different devices: /device:TPU:24 before, /device:TPU:1 now
where the time goes in v1:
time: 104 us; the launch traced here: 103 us
  Pallas kernels  100 us (96%)
  local copies, waits for them, and re-layouts  2.49 us (2%)
    pallas_call x1, Pallas kernels, local(): pl.pallas_call(functools.partial(kernel, sections, heads), out_shape=jax....  100 us
    unnamed x5, local copies, waits for them, and re-layouts  2.49 us

profile of v1, /device:TPU:1, one launch (start us, length us, event | category | flops | bytes accessed | tf_op | source)
XLA Modules:
  0.0 103.4 jit_solution(16717928287454203728)
XLA Ops:
  0.7 0.0 copy-start
  0.7 1.0 copy-done
  1.7 0.0 copy-start.1
  1.7 0.7 copy-done.1
  2.4 100.3 %relay.1 = bf16[256,896]{1,0:T(8,128)(2,1)S(1)} custom-call(bf16[256,896]{1,0:T(8,128)(2,1)S(1)} %bitcast.4, bf16[3,1792,896]{2,1,0:T(8,128)(2,1)} %bitcast.5, bf16[1,3584]{1,0:T(2,128)(2,1)S(1)} %copy-done.1, s32[1]{0:T(128)S(6)} %copy.6.pre_ref), custom_call_target="tpu_custom_call" | custom-call | flops 9865003008 | bytes 9633792 | tf_op jit(solution)/shard_map/relay/pallas_call | solution.py:326
  102.6 0.8 copy.7
Async XLA Ops:
  0.7 1.0 copy-start
  1.7 0.7 copy-start.1

commit v2 on v0

v2 whole, which is shorter than its diff:
```python
import functools
import math

import jax
import jax.numpy as jnp
from jax import lax
from jax.experimental import pallas as pl
from jax.experimental.pallas import tpu as pltpu
from jax.sharding import PartitionSpec as P

HD = 128
BLOCKS = 2
PIECES = 2
AHEAD = 4
SEND_AT = 0
MESH = pl.DeviceIdType.MESH


def kernel(
    sections,
    heads,
    a_hbm,
    w_hbm,
    gain_hbm,
    pre_ref,
    out_ref,
    w,
    feats,
    psend,
    precv,
    a_own,
    x_prev,
    own,
    gain,
    keys,
    values,
    squares,
    scale,
    note,
    heard,
    w_sem,
    in_sem,
    q_send,
    q_recv,
    p_send,
    p_recv,
    s_send,
    s_recv,
    part_send,
    part_recv,
    hop_send,
    hop_recv,
    note_send,
    note_recv,
):
    s, d, t = lax.axis_index("section"), lax.axis_index("dp"), lax.axis_index("tensor")
    high, core = t // 2, t % 2
    width = a_own.shape[1]
    rows = a_own.shape[0] // BLOCKS
    features = 4 * width
    stages = 2 * BLOCKS

    partner = (s, 1 - d, t)
    other = (s, 1 - d, (1 - high) * 2 + core)
    sibling = (s, d, high * 2 + 1 - core)
    opposite = (s, d, (1 - high) * 2 + core)
    after = (lax.rem(s + 1, sections), d, t)
    before = (lax.rem(s + sections - 1, sections), d, t)

    straight = high == d
    crossed = jnp.logical_not(straight)
    mine = jnp.where(straight, 1, 3)
    to_partner = jnp.where(straight, 2, 0)
    from_partner = jnp.where(straight, 0, 2)

    def head_columns(h):
        return pl.ds(pl.multiple_of(h * HD, HD), HD)

    def tokens(block):
        return pl.ds(block * rows, rows)

    def piece_rows(r):
        return pl.ds(pl.multiple_of(r * (rows // PIECES), rows // PIECES), rows // PIECES)

    def piece(stage, slot, c, r):
        return feats.at[stage, slot, c, piece_rows(r)]

    def remote(src, dst, send, recv, device):
        return pltpu.make_async_remote_copy(
            src_ref=src, dst_ref=dst, send_sem=send, recv_sem=recv, device_id=device, device_id_type=MESH
        )

    def partner_copy(stage, r):
        return remote(
            piece(stage, mine, core, r), piece(stage, to_partner, core, r),
            p_send.at[stage, r], p_recv.at[stage, r], partner,
        )

    def partner_arrival(stage, r):
        there = piece(stage, from_partner, core, r)
        return remote(there, there, p_send.at[stage, r], p_recv.at[stage, r], partner)

    def other_copy(stage, slot, r):
        return remote(
            piece(stage, 3 - slot, core, r), piece(stage, slot, core, r),
            q_send.at[stage, slot, r], q_recv.at[stage, slot, r], other,
        )

    def other_arrival(stage, slot, r):
        there = piece(stage, slot, core, r)
        return remote(there, there, q_send.at[stage, slot, r], q_recv.at[stage, slot, r], other)

    def sibling_copy(stage, slot, h):
        here = piece(stage, slot, core, h)
        return remote(here, here, s_send.at[stage, slot, h], s_recv.at[stage, slot, h], sibling)

    def sibling_arrival(stage, slot, h):
        there = piece(stage, slot, 1 - core, h)
        return remote(there, there, s_send.at[stage, slot, h], s_recv.at[stage, slot, h], sibling)

    def part_copy(stage, g):
        return remote(
            psend.at[stage, g], precv.at[stage, g], part_send.at[stage, g], part_recv.at[stage, g], partner
        )

    def hop_copy(block, h):
        here = (tokens(block), head_columns(h))
        return remote(own.at[here], x_prev.at[here], hop_send.at[block, h], hop_recv.at[block, h], after)

    def note_copy(stage, i):
        return remote(
            note.at[stage, i], heard.at[stage, i], note_send.at[stage, i], note_recv.at[stage, i],
            (sibling, opposite)[i],
        )

    def w_copy(g, j):
        return pltpu.make_async_copy(
            w_hbm.at[j, :, head_columns(g)], w.at[g, :, pl.ds(j * HD, HD)], w_sem.at[g, j]
        )

    a_copy = pltpu.make_async_copy(a_hbm, a_own, in_sem.at[0])
    gain_copy = pltpu.make_async_copy(gain_hbm, gain, in_sem.at[1])
    a_copy.start()
    gain_copy.start()

    @pl.loop(0, heads)
    def _(g):
        for j in range(3):
            w_copy(g, j).start()

    barrier = pltpu.get_barrier_semaphore()
    for device in (partner, other, sibling, opposite, before):
        pl.semaphore_signal(barrier, inc=1, device_id=device, device_id_type=MESH)

    @pl.when(s == 0)
    def _():
        x_prev[...] = jnp.zeros_like(x_prev)

    a_copy.wait()
    gain_copy.wait()
    pl.semaphore_wait(barrier, 5)

    def layer_input(stage, where):
        if stage < BLOCKS:
            return a_own[where].astype(jnp.float32)
        return x_prev[where].astype(jnp.float32)

    def send_pieces(stage):
        block = stage % BLOCKS
        if stage >= BLOCKS:

            @pl.when(s > 0)
            def _():
                @pl.loop(0, heads)
                def _(h):
                    hop_copy(block, h).wait_recv()

        row = gain[0:1, pl.ds(pl.multiple_of(t * width, HD), width)].astype(jnp.float32)

        @pl.loop(0, PIECES)
        def _(r):
            first = pl.multiple_of(block * rows + r * (rows // PIECES), rows // PIECES)
            x = layer_input(stage, (pl.ds(first, rows // PIECES), slice(None)))
            feats[stage, mine, core, piece_rows(r)] = (x * row).astype(jnp.bfloat16)
            partner_copy(stage, r).start()

            @pl.when(straight)
            def _():
                sibling_copy(stage, 1, r).start()

            @pl.when(crossed)
            def _():
                other_copy(stage, 0, r).start()

            x = x * x
            squares[piece_rows(r)] = sum(x[:, h * HD : (h + 1) * HD] for h in range(heads))

        sums = jnp.sum(squares[...], axis=1, keepdims=True)
        note[stage, 0] = jnp.broadcast_to(sums, (rows, HD)).T[0:8, :]
        note_copy(stage, 0).start()

    def pass_on(stage):
        @pl.when(straight)
        def _():
            @pl.loop(0, PIECES)
            def _(r):
                partner_arrival(stage, r).wait_recv()
                sibling_copy(stage, 0, r).start()

        @pl.when(crossed)
        def _():
            @pl.loop(0, PIECES)
            def _(r):
                other_arrival(stage, 0, r).wait_recv()
                sibling_copy(stage, 0, r).start()
                partner_arrival(stage, r).wait_recv()
                other_copy(stage, 1, r).start()

    def other_sequence(stage):
        note_copy(stage, 0).wait_recv()
        note[stage, 1] = note[stage, 0] + heard[stage, 0]
        note_copy(stage, 1).start()

        @pl.loop(0, PIECES)
        def _(r):
            sibling_arrival(stage, 0, r).wait_recv()

    def late_pieces(stage):
        @pl.when(crossed)
        def _():
            @pl.loop(0, PIECES)
            def _(r):
                other_arrival(stage, 1, r).wait_recv()
                sibling_copy(stage, 1, r).start()

        note_copy(stage, 1).wait_recv()
        total = note[stage, 1] + heard[stage, 1]
        inverse = lax.rsqrt(total * (1.0 / features) + 1e-05)
        scale[...] = jnp.broadcast_to(inverse[0:1, :], (HD, rows)).T

        @pl.loop(0, PIECES)
        def _(r):
            sibling_arrival(stage, 1, r).wait_recv()

    def project(stage, slot, g):
        return sum(
            jnp.dot(feats[stage, slot, c], w[g, c * width : (c + 1) * width], preferred_element_type=jnp.float32)
            for c in range(2)
        )

    def send_part(stage, g):
        part = project(stage, 0, g)
        psend[stage, g] = part.astype(jnp.bfloat16)
        part_copy(stage, g).start()

    def attend(stage, g):
        block = stage % BLOCKS
        part = project(stage, 1, g)
        part_copy(stage, g).wait_recv()
        part = part + precv[stage, g].astype(jnp.float32)
        inverse = scale[...]
        query = (part[:, 0:HD] * inverse).astype(jnp.bfloat16)
        keys[g, tokens(block)] = (part[:, HD : 2 * HD] * inverse).astype(jnp.bfloat16)
        values[g, tokens(block)] = (part[:, 2 * HD :] * inverse).astype(jnp.bfloat16)
        seen = (block + 1) * rows
        scores = lax.dot_general(
            query, keys[g, 0:seen], (((1,), (1,)), ((), ())), preferred_element_type=jnp.float32
        ) * (1.0 / math.sqrt(HD))
        causal = lax.broadcasted_iota(jnp.int32, (rows, seen), 0) + block * rows >= lax.broadcasted_iota(
            jnp.int32, (rows, seen), 1
        )
        scores = jnp.where(causal, scores, jnp.float32(-1e30))
        powers = jnp.exp(scores - jnp.max(scores, axis=1, keepdims=True))
        chance = (powers * (1.0 / jnp.sum(powers, axis=1, keepdims=True))).astype(jnp.bfloat16)
        mixture = jnp.dot(chance, values[g, 0:seen], preferred_element_type=jnp.float32)
        return (layer_input(stage, (tokens(block), head_columns(g))) + mixture).astype(jnp.bfloat16)

    send_pieces(0)
    send_pieces(1)
    pass_on(0)

    other_sequence(0)

    @pl.loop(0, heads)
    def _(g):
        for j in range(3):
            w_copy(g, j).wait()

        @pl.when(g < AHEAD)
        def _():
            send_part(0, g)

    pass_on(1)
    other_sequence(1)
    take = pre_ref[0] == 1

    for stage in range(stages):
        layer, block = stage // BLOCKS, stage % BLOCKS
        late_pieces(stage)
        feeds = 1 <= stage < stages - 1

        @pl.loop(0, heads)
        def _(g):
            if feeds:

                @pl.when(g == heads - AHEAD)
                def _():
                    pass_on(stage + 1)
                    other_sequence(stage + 1)

            here = (tokens(block), head_columns(g))
            result = attend(stage, g)
            if layer == 0:
                own[here] = result

                @pl.when(s < sections - 1)
                def _():
                    hop_copy(block, g).start()

            else:
                out_ref[here] = jnp.where(take, result, own[here])

            coming = g + AHEAD
            if stage < stages - 1:
                send_part(stage + coming // heads, lax.rem(coming, heads))
            else:

                @pl.when(coming < heads)
                def _():
                    send_part(stage, coming)

            if feeds:

                @pl.when(g == SEND_AT)
                def _():
                    send_pieces(stage + 1)

    for stage in range(stages):

        @pl.loop(0, PIECES)
        def _(r):
            partner_copy(stage, r).wait_send()

            @pl.when(crossed)
            def _():
                other_copy(stage, 0, r).wait_send()
                other_copy(stage, 1, r).wait_send()

            sibling_copy(stage, 0, r).wait_send()
            sibling_copy(stage, 1, r).wait_send()

        @pl.loop(0, heads)
        def _(h):
            part_copy(stage, h).wait_send()
            if stage < BLOCKS:

                @pl.when(s < sections - 1)
                def _():
                    hop_copy(stage, h).wait_send()

        for i in range(2):
            note_copy(stage, i).wait_send()


def local(sections, inputs, qkv_weight, norm_gain, preempted):
    rows, width = inputs.shape[2:]
    heads = width // HD
    depth = qkv_weight.shape[2]
    stages, short = 2 * BLOCKS, rows // BLOCKS
    bf16, f32 = jnp.bfloat16, jnp.float32
    dma = pltpu.SemaphoreType.DMA
    hbm = pl.BlockSpec(memory_space=pltpu.HBM)
    result = pl.pallas_call(
        functools.partial(kernel, sections, heads),
        out_shape=jax.ShapeDtypeStruct((rows, width), bf16),
        in_specs=[hbm, hbm, hbm, pl.BlockSpec(memory_space=pltpu.SMEM)],
        out_specs=pl.BlockSpec(memory_space=pltpu.VMEM),
        scratch_shapes=[
            pltpu.VMEM((heads, depth, 3 * HD), bf16),
            pltpu.VMEM((stages, 4, 2, short, width), bf16),
            pltpu.VMEM((stages, heads, short, 3 * HD), bf16),
            pltpu.VMEM((stages, heads, short, 3 * HD), bf16),
            pltpu.VMEM((rows, width), bf16),
            pltpu.VMEM((rows, width), bf16),
            pltpu.VMEM((rows, width), bf16),
            pltpu.VMEM((1, 4 * width), bf16),
            pltpu.VMEM((heads, rows, HD), bf16),
            pltpu.VMEM((heads, rows, HD), bf16),
            pltpu.VMEM((short, HD), f32),
            pltpu.VMEM((short, HD), f32),
            pltpu.VMEM((stages, 2, 8, short), f32),
            pltpu.VMEM((stages, 2, 8, short), f32),
            dma((heads, 3)),
            dma((2,)),
            dma((stages, 2, PIECES)),
            dma((stages, 2, PIECES)),
            dma((stages, PIECES)),
            dma((stages, PIECES)),
            dma((stages, 2, PIECES)),
            dma((stages, 2, PIECES)),
            dma((stages, heads)),
            dma((stages, heads)),
            dma((BLOCKS, heads)),
            dma((BLOCKS, heads)),
            dma((stages, 2)),
            dma((stages, 2)),
        ],
        compiler_params=pltpu.CompilerParams(
            collective_id=0, has_side_effects=True, vmem_limit_bytes=55900000
        ),
        cost_estimate=pl.CostEstimate(
            flops=8 * rows * depth * 3 * width, bytes_accessed=qkv_weight.size * 2, transcendentals=0
        ),
        name="relay",
    )(inputs[0, 0], qkv_weight[0], norm_gain, preempted)
    return result[None, None]


def solution(mesh):
    placed = (
        P("section", "dp", None, "tensor"),
        P("section", None, "dp", "tensor"),
        P("section", None),
        P("section"),
    )
    return jax.shard_map(
        functools.partial(local, mesh.shape["section"]),
        mesh=mesh,
        in_specs=placed,
        out_specs=P("section", "dp", None, "tensor"),
        check_vma=False,
    )
```

time: 344 us -> 91.1 us (0.26)
  waiting for transfers between devices: 218 us -> 0 us
  Pallas kernels: 0 us -> 87.6 us
  blocking collectives: 50.5 us -> 0 us
  matrix products: 29.6 us -> 0 us
  other arithmetic: 13.3 us -> 0 us
  between operations: 13.9 us -> 0.67 us
  local copies, waits for them, and re-layouts: 12.7 us -> 1.48 us
  starting transfers between devices: 3.59 us -> 0 us
    reduce_scatter x2 -> x0, waiting for transfers between devices: 145 us -> none  [project(): lax.psum_scatter(jnp.einsum('rd,kde->rke', all_rows, weight, preferred_el...]
    pallas_call x0 -> x1, Pallas kernels: none -> 87.6 us  [local(): pl.pallas_call(functools.partial(kernel, sections, heads), out_shape=jax....]
    all_gather x2 -> x0, waiting for transfers between devices: 59.5 us -> none  [gather_rows(): return lax.all_gather(hidden_in, 'tensor', axis=2, tiled=True)]
    all_to_all x2 -> x0, blocking collectives: 50.5 us -> none  [project(): lax.all_to_all(normed, 'dp', split_axis=1, concat_axis=0, tiled=True)]
    dot_general x4 -> x0, matrix products: 25.6 us -> none  [the longest x2 22 us: project(): jnp.einsum('rd,kde->rke', all_rows, weight, preferred_element_type=jnp.fl...]
    ppermute x1 -> x0, waiting for transfers between devices: 12.8 us -> none  [from_behind(): return lax.ppermute(array, axis, pairs)]
    all_to_all x4 -> x0, local copies, waits for them, and re-layouts: 8.45 us -> none  [project(): lax.all_to_all(normed, 'dp', split_axis=1, concat_axis=0, tiled=True)]
    convert_element_type x6 -> x0, other arithmetic: 8.23 us -> none  [the longest x3 4.31 us: attend(): normed = (float_acts * inverse_rms * gain_row).astype(jnp.bfloat16)]
  transfers between devices with their start and end apart: 5 -> 0, of which waited for: 5 -> 0; matrix products, arithmetic and copies ran while one was open for 0% -> 0% of each run, Pallas kernels for 0% -> 0%
where the time goes in v2:
time: 91.1 us; the launch traced here: 89.7 us
  Pallas kernels  87.6 us (96%)
  local copies, waits for them, and re-layouts  1.48 us (2%)
    pallas_call x1, Pallas kernels, local(): pl.pallas_call(functools.partial(kernel, sections, heads), out_shape=jax....  87.6 us

profile of v2, /device:TPU:24, one launch (start us, length us, event | category | flops | bytes accessed | tf_op | source)
XLA Modules:
  0.0 89.7 jit_solution(1857520487165972234)
XLA Ops:
  0.7 0.0 copy-start
  0.7 0.7 copy-done
  1.4 87.6 %relay.1 = bf16[256,896]{1,0:T(8,128)(2,1)S(1)} custom-call(bf16[256,896]{1,0:T(8,128)(2,1)} %bitcast.5, bf16[3,1792,896]{2,1,0:T(8,128)(2,1)} %bitcast.4, bf16[1,3584]{1,0:T(2,128)(2,1)S(1)} %copy-done, s32[1]{0:T(128)S(6)} %copy.6.pre_ref), custom_call_target="tpu_custom_call" | custom-call | flops 9865003008 | bytes 9633792 | tf_op jit(solution)/shard_map/relay/pallas_call | solution.py:373
  89.0 0.8 copy.7
Async XLA Ops:
  0.7 0.7 copy-start

commit v3 on v2

--- a/solution.py
+++ b/solution.py
@@ -13,6 +13,8 @@
 PIECES = 2
 AHEAD = 4
 SEND_AT = 0
+DRAIN_AT = 5
+COLUMN = 8
 MESH = pl.DeviceIdType.MESH
 
 
@@ -52,6 +54,7 @@
     hop_recv,
     note_send,
     note_recv,
+    ready,
 ):
     s, d, t = lax.axis_index("section"), lax.axis_index("dp"), lax.axis_index("tensor")
     high, core = t // 2, t % 2
@@ -118,9 +121,10 @@
         there = piece(stage, slot, 1 - core, h)
         return remote(there, there, s_send.at[stage, slot, h], s_recv.at[stage, slot, h], sibling)
 
-    def part_copy(stage, g):
+    def part_copy(stage, g, i):
+        here = (stage, g, slice(None), (pl.ds(0, 2 * HD), pl.ds(2 * HD, HD))[i])
         return remote(
-            psend.at[stage, g], precv.at[stage, g], part_send.at[stage, g], part_recv.at[stage, g], partner
+            psend.at[here], precv.at[here], part_send.at[i, stage, g], part_recv.at[i, stage, g], partner
         )
 
     def hop_copy(block, h):
@@ -138,109 +142,139 @@
             w_hbm.at[j, :, head_columns(g)], w.at[g, :, pl.ds(j * HD, HD)], w_sem.at[g, j]
         )
 
+    barrier = pltpu.get_barrier_semaphore()
+    for device in (partner, other, sibling, opposite):
+        pl.semaphore_signal(barrier, inc=1, device_id=device, device_id_type=MESH)
+
+    first, last = s % COLUMN == 0, s % COLUMN == COLUMN - 1
+
+    @pl.when(first & (s > 0))
+    def _():
+        pl.semaphore_signal(barrier, inc=1, device_id=before, device_id_type=MESH)
+
+    @pl.when(jnp.logical_not(last))
+    def _():
+        pl.semaphore_signal(barrier, inc=1, device_id=after, device_id_type=MESH)
+
     a_copy = pltpu.make_async_copy(a_hbm, a_own, in_sem.at[0])
     gain_copy = pltpu.make_async_copy(gain_hbm, gain, in_sem.at[1])
     a_copy.start()
     gain_copy.start()
 
-    @pl.loop(0, heads)
-    def _(g):
-        for j in range(3):
-            w_copy(g, j).start()
-
-    barrier = pltpu.get_barrier_semaphore()
-    for device in (partner, other, sibling, opposite, before):
-        pl.semaphore_signal(barrier, inc=1, device_id=device, device_id_type=MESH)
-
     @pl.when(s == 0)
     def _():
         x_prev[...] = jnp.zeros_like(x_prev)
 
     a_copy.wait()
     gain_copy.wait()
-    pl.semaphore_wait(barrier, 5)
+    pl.semaphore_wait(
+        barrier, 4 + jnp.where(first, 0, 1) + jnp.where(last & (s < sections - 1), 1, 0)
+    )
+
+    @pl.when(jnp.logical_not(first))
+    def _():
+        pl.semaphore_signal(ready, inc=1, device_id=before, device_id_type=MESH)
 
     def layer_input(stage, where):
         if stage < BLOCKS:
             return a_own[where].astype(jnp.float32)
         return x_prev[where].astype(jnp.float32)
 
+    def traveling(stage):
+        return pl.when(s > 0) if stage >= BLOCKS else (lambda step: step())
+
     def send_pieces(stage):
         block = stage % BLOCKS
         if stage >= BLOCKS:
 
-            @pl.when(s > 0)
+            @pl.when(s == 0)
             def _():
+                squares[...] = jnp.zeros_like(squares)
+                for slot in range(2):
+                    feats[stage, slot] = jnp.zeros(feats.shape[2:], feats.dtype)
+
+        @traveling(stage)
+        def _():
+            if stage >= BLOCKS:
+
                 @pl.loop(0, heads)
                 def _(h):
                     hop_copy(block, h).wait_recv()
 
-        row = gain[0:1, pl.ds(pl.multiple_of(t * width, HD), width)].astype(jnp.float32)
-
-        @pl.loop(0, PIECES)
-        def _(r):
-            first = pl.multiple_of(block * rows + r * (rows // PIECES), rows // PIECES)
-            x = layer_input(stage, (pl.ds(first, rows // PIECES), slice(None)))
-            feats[stage, mine, core, piece_rows(r)] = (x * row).astype(jnp.bfloat16)
-            partner_copy(stage, r).start()
-
-            @pl.when(straight)
-            def _():
-                sibling_copy(stage, 1, r).start()
-
-            @pl.when(crossed)
-            def _():
-                other_copy(stage, 0, r).start()
-
-            x = x * x
-            squares[piece_rows(r)] = sum(x[:, h * HD : (h + 1) * HD] for h in range(heads))
+            row = gain[0:1, pl.ds(pl.multiple_of(t * width, HD), width)].astype(jnp.float32)
+
+            @pl.loop(0, PIECES)
+            def _(r):
+                first = pl.multiple_of(block * rows + r * (rows // PIECES), rows // PIECES)
+                x = layer_input(stage, (pl.ds(first, rows // PIECES), slice(None)))
+                feats[stage, mine, core, piece_rows(r)] = (x * row).astype(jnp.bfloat16)
+                partner_copy(stage, r).start()
+
+                @pl.when(straight)
+                def _():
+                    sibling_copy(stage, 1, r).start()
+
+                @pl.when(crossed)
+                def _():
+                    other_copy(stage, 0, r).start()
+
+                x = x * x
+                squares[piece_rows(r)] = sum(x[:, h * HD : (h + 1) * HD] for h in range(heads))
 
         sums = jnp.sum(squares[...], axis=1, keepdims=True)
         note[stage, 0] = jnp.broadcast_to(sums, (rows, HD)).T[0:8, :]
         note_copy(stage, 0).start()
 
     def pass_on(stage):
-        @pl.when(straight)
-        def _():
-            @pl.loop(0, PIECES)
-            def _(r):
-                partner_arrival(stage, r).wait_recv()
-                sibling_copy(stage, 0, r).start()
-
-        @pl.when(crossed)
-        def _():
-            @pl.loop(0, PIECES)
-            def _(r):
-                other_arrival(stage, 0, r).wait_recv()
-                sibling_copy(stage, 0, r).start()
-                partner_arrival(stage, r).wait_recv()
-                other_copy(stage, 1, r).start()
+        @traveling(stage)
+        def _():
+            @pl.when(straight)
+            def _():
+                @pl.loop(0, PIECES)
+                def _(r):
+                    partner_arrival(stage, r).wait_recv()
+                    sibling_copy(stage, 0, r).start()
+
+            @pl.when(crossed)
+            def _():
+                @pl.loop(0, PIECES)
+                def _(r):
+                    other_arrival(stage, 0, r).wait_recv()
+                    sibling_copy(stage, 0, r).start()
+                    partner_arrival(stage, r).wait_recv()
+                    other_copy(stage, 1, r).start()
 
     def other_sequence(stage):
         note_copy(stage, 0).wait_recv()
         note[stage, 1] = note[stage, 0] + heard[stage, 0]
         note_copy(stage, 1).start()
 
-        @pl.loop(0, PIECES)
-        def _(r):
-            sibling_arrival(stage, 0, r).wait_recv()
-
-    def late_pieces(stage):
-        @pl.when(crossed)
+        @traveling(stage)
         def _():
             @pl.loop(0, PIECES)
             def _(r):
-                other_arrival(stage, 1, r).wait_recv()
-                sibling_copy(stage, 1, r).start()
+                sibling_arrival(stage, 0, r).wait_recv()
+
+    def late_pieces(stage):
+        @traveling(stage)
+        def _():
+            @pl.when(crossed)
+            def _():
+                @pl.loop(0, PIECES)
+                def _(r):
+                    other_arrival(stage, 1, r).wait_recv()
+                    sibling_copy(stage, 1, r).start()
 
         note_copy(stage, 1).wait_recv()
         total = note[stage, 1] + heard[stage, 1]
         inverse = lax.rsqrt(total * (1.0 / features) + 1e-05)
         scale[...] = jnp.broadcast_to(inverse[0:1, :], (HD, rows)).T
 
-        @pl.loop(0, PIECES)
-        def _(r):
-            sibling_arrival(stage, 1, r).wait_recv()
+        @traveling(stage)
+        def _():
+            @pl.loop(0, PIECES)
+            def _(r):
+                sibling_arrival(stage, 1, r).wait_recv()
 
     def project(stage, slot, g):
         return sum(
@@ -251,17 +285,18 @@
     def send_part(stage, g):
         part = project(stage, 0, g)
         psend[stage, g] = part.astype(jnp.bfloat16)
-        part_copy(stage, g).start()
+        for i in range(2):
+            part_copy(stage, g, i).start()
 
     def attend(stage, g):
         block = stage % BLOCKS
         part = project(stage, 1, g)
-        part_copy(stage, g).wait_recv()
-        part = part + precv[stage, g].astype(jnp.float32)
+        part_copy(stage, g, 0).wait_recv()
         inverse = scale[...]
-        query = (part[:, 0:HD] * inverse).astype(jnp.bfloat16)
-        keys[g, tokens(block)] = (part[:, HD : 2 * HD] * inverse).astype(jnp.bfloat16)
-        values[g, tokens(block)] = (part[:, 2 * HD :] * inverse).astype(jnp.bfloat16)
+        query = (part[:, 0:HD] + precv[stage, g, :, 0:HD].astype(jnp.float32)) * inverse
+        key = (part[:, HD : 2 * HD] + precv[stage, g, :, HD : 2 * HD].astype(jnp.float32)) * inverse
+        query = query.astype(jnp.bfloat16)
+        keys[g, tokens(block)] = key.astype(jnp.bfloat16)
         seen = (block + 1) * rows
         scores = lax.dot_general(
             query, keys[g, 0:seen], (((1,), (1,)), ((), ())), preferred_element_type=jnp.float32
@@ -272,10 +307,44 @@
         scores = jnp.where(causal, scores, jnp.float32(-1e30))
         powers = jnp.exp(scores - jnp.max(scores, axis=1, keepdims=True))
         chance = (powers * (1.0 / jnp.sum(powers, axis=1, keepdims=True))).astype(jnp.bfloat16)
+        part_copy(stage, g, 1).wait_recv()
+        value = (part[:, 2 * HD :] + precv[stage, g, :, 2 * HD :].astype(jnp.float32)) * inverse
+        values[g, tokens(block)] = value.astype(jnp.bfloat16)
         mixture = jnp.dot(chance, values[g, 0:seen], preferred_element_type=jnp.float32)
         return (layer_input(stage, (tokens(block), head_columns(g))) + mixture).astype(jnp.bfloat16)
 
+    def sent(stage):
+        @traveling(stage)
+        def _():
+            @pl.loop(0, PIECES)
+            def _(r):
+                partner_copy(stage, r).wait_send()
+
+                @pl.when(crossed)
+                def _():
+                    other_copy(stage, 0, r).wait_send()
+                    other_copy(stage, 1, r).wait_send()
+
+                sibling_copy(stage, 0, r).wait_send()
+                sibling_copy(stage, 1, r).wait_send()
+
+        for i in range(2):
+            note_copy(stage, i).wait_send()
+
+    def hops_sent(block):
+        @pl.when(s < sections - 1)
+        def _():
+            @pl.loop(0, heads)
+            def _(h):
+                hop_copy(block, h).wait_send()
+
     send_pieces(0)
+
+    @pl.loop(0, heads)
+    def _(g):
+        for j in range(3):
+            w_copy(g, j).start()
+
     send_pieces(1)
     pass_on(0)
 
@@ -292,6 +361,11 @@
 
     pass_on(1)
     other_sequence(1)
+
+    @pl.when(jnp.logical_not(last))
+    def _():
+        pl.semaphore_wait(ready, 1)
+
     take = pre_ref[0] == 1
 
     for stage in range(stages):
@@ -308,6 +382,21 @@
                     pass_on(stage + 1)
                     other_sequence(stage + 1)
 
+            coming = g + AHEAD
+            if stage < stages - 1:
+                send_part(stage + coming // heads, lax.rem(coming, heads))
+            else:
+
+                @pl.when(coming < heads)
+                def _():
+                    send_part(stage, coming)
+
+            @pl.when(g == DRAIN_AT)
+            def _():
+                sent(stage)
+                if layer > 0:
+                    hops_sent(block)
+
             here = (tokens(block), head_columns(g))
             result = attend(stage, g)
             if layer == 0:
@@ -320,46 +409,14 @@
             else:
                 out_ref[here] = jnp.where(take, result, own[here])
 
-            coming = g + AHEAD
-            if stage < stages - 1:
-                send_part(stage + coming // heads, lax.rem(coming, heads))
-            else:
-
-                @pl.when(coming < heads)
-                def _():
-                    send_part(stage, coming)
+            for i in range(2):
+                part_copy(stage, g, i).wait_send()
 
             if feeds:
 
                 @pl.when(g == SEND_AT)
                 def _():
                     send_pieces(stage + 1)
-
-    for stage in range(stages):
-
-        @pl.loop(0, PIECES)
-        def _(r):
-            partner_copy(stage, r).wait_send()
-
-            @pl.when(crossed)
-            def _():
-                other_copy(stage, 0, r).wait_send()
-                other_copy(stage, 1, r).wait_send()
-
-            sibling_copy(stage, 0, r).wait_send()
-            sibling_copy(stage, 1, r).wait_send()
-
-        @pl.loop(0, heads)
-        def _(h):
-            part_copy(stage, h).wait_send()
-            if stage < BLOCKS:
-
-                @pl.when(s < sections - 1)
-                def _():
-                    hop_copy(stage, h).wait_send()
-
-        for i in range(2):
-            note_copy(stage, i).wait_send()
 
 
 def local(sections, inputs, qkv_weight, norm_gain, preempted):
@@ -370,6 +427,7 @@
     bf16, f32 = jnp.bfloat16, jnp.float32
     dma = pltpu.SemaphoreType.DMA
     hbm = pl.BlockSpec(memory_space=pltpu.HBM)
+    operands = (inputs[0, 0], qkv_weight[0], norm_gain)
     result = pl.pallas_call(
         functools.partial(kernel, sections, heads),
         out_shape=jax.ShapeDtypeStruct((rows, width), bf16),
@@ -398,21 +456,22 @@
             dma((stages, PIECES)),
             dma((stages, 2, PIECES)),
             dma((stages, 2, PIECES)),
-            dma((stages, heads)),
-            dma((stages, heads)),
+            dma((2, stages, heads)),
+            dma((2, stages, heads)),
             dma((BLOCKS, heads)),
             dma((BLOCKS, heads)),
             dma((stages, 2)),
             dma((stages, 2)),
+            pltpu.SemaphoreType.REGULAR,
         ],
         compiler_params=pltpu.CompilerParams(
-            collective_id=0, has_side_effects=True, vmem_limit_bytes=55900000
+            collective_id=0, has_side_effects=True, vmem_limit_bytes=48 * 2**20
         ),
         cost_estimate=pl.CostEstimate(
             flops=8 * rows * depth * 3 * width, bytes_accessed=qkv_weight.size * 2, transcendentals=0
         ),
         name="relay",
-    )(inputs[0, 0], qkv_weight[0], norm_gain, preempted)
+    )(*(pltpu.with_memory_space_constraint(x, pltpu.HBM) for x in operands), preempted)
     return result[None, None]
 
 

time: 91.1 us -> 88.2 us (0.968); the launches traced: 89.7 us -> 88.1 us
  no operation moved by 1% of the time
where the time goes in v3:
time: 88.2 us; the launch traced here: 88.1 us
  Pallas kernels  86.7 us (98%)
    pallas_call x1, Pallas kernels, local(): pl.pallas_call(functools.partial(kernel, sections, heads), out_shape=jax....  86.7 us

profile of v3, /device:TPU:24, one launch (start us, length us, event | category | flops | bytes accessed | tf_op | source)
XLA Modules:
  0.0 88.1 jit_solution(7428903486535374317)
XLA Ops:
  0.7 86.7 %relay.1 = bf16[256,896]{1,0:T(8,128)(2,1)S(1)} custom-call(bf16[256,896]{1,0:T(8,128)(2,1)} %bitcast.5, bf16[3,1792,896]{2,1,0:T(8,128)(2,1)} %bitcast.4, bf16[1,3584]{1,0:T(2,128)(2,1)} %gain_hbm.1, s32[1]{0:T(128)S(6)} %copy.6.pre_ref), custom_call_target="tpu_custom_call" | custom-call | flops 9865003008 | bytes 9633792 | tf_op jit(solution)/shard_map/relay/pallas_call | solution.py:431
  87.3 0.8 copy.7

commit v4 on v3

--- a/solution.py
+++ b/solution.py
@@ -10,10 +10,10 @@
 
 HD = 128
 BLOCKS = 2
-PIECES = 2
+PIECES = 1
 AHEAD = 4
-SEND_AT = 0
-DRAIN_AT = 5
+SEND_AT = 1
+PASS_AT = 4
 COLUMN = 8
 MESH = pl.DeviceIdType.MESH
 
@@ -142,9 +142,19 @@
             w_hbm.at[j, :, head_columns(g)], w.at[g, :, pl.ds(j * HD, HD)], w_sem.at[g, j]
         )
 
+    def a_copy(block):
+        return pltpu.make_async_copy(a_hbm.at[tokens(block)], a_own.at[tokens(block)], in_sem.at[block])
+
+    gain_copy = pltpu.make_async_copy(gain_hbm, gain, in_sem.at[BLOCKS])
+    a_copy(0).start()
+    gain_copy.start()
     barrier = pltpu.get_barrier_semaphore()
-    for device in (partner, other, sibling, opposite):
+    for device in (opposite, partner, sibling):
         pl.semaphore_signal(barrier, inc=1, device_id=device, device_id_type=MESH)
+
+    @pl.when(crossed)
+    def _():
+        pl.semaphore_signal(barrier, inc=1, device_id=other, device_id_type=MESH)
 
     first, last = s % COLUMN == 0, s % COLUMN == COLUMN - 1
 
@@ -156,24 +166,12 @@
     def _():
         pl.semaphore_signal(barrier, inc=1, device_id=after, device_id_type=MESH)
 
-    a_copy = pltpu.make_async_copy(a_hbm, a_own, in_sem.at[0])
-    gain_copy = pltpu.make_async_copy(gain_hbm, gain, in_sem.at[1])
-    a_copy.start()
-    gain_copy.start()
+    for block in range(1, BLOCKS):
+        a_copy(block).start()
 
     @pl.when(s == 0)
     def _():
         x_prev[...] = jnp.zeros_like(x_prev)
-
-    a_copy.wait()
-    gain_copy.wait()
-    pl.semaphore_wait(
-        barrier, 4 + jnp.where(first, 0, 1) + jnp.where(last & (s < sections - 1), 1, 0)
-    )
-
-    @pl.when(jnp.logical_not(first))
-    def _():
-        pl.semaphore_signal(ready, inc=1, device_id=before, device_id_type=MESH)
 
     def layer_input(stage, where):
         if stage < BLOCKS:
@@ -183,7 +181,7 @@
     def traveling(stage):
         return pl.when(s > 0) if stage >= BLOCKS else (lambda step: step())
 
-    def send_pieces(stage):
+    def make_pieces(stage):
         block = stage % BLOCKS
         if stage >= BLOCKS:
 
@@ -208,22 +206,26 @@
                 first = pl.multiple_of(block * rows + r * (rows // PIECES), rows // PIECES)
                 x = layer_input(stage, (pl.ds(first, rows // PIECES), slice(None)))
                 feats[stage, mine, core, piece_rows(r)] = (x * row).astype(jnp.bfloat16)
-                partner_copy(stage, r).start()
-
-                @pl.when(straight)
-                def _():
-                    sibling_copy(stage, 1, r).start()
-
-                @pl.when(crossed)
-                def _():
-                    other_copy(stage, 0, r).start()
-
+                if stage >= BLOCKS:
+                    send_piece(stage, r)
                 x = x * x
                 squares[piece_rows(r)] = sum(x[:, h * HD : (h + 1) * HD] for h in range(heads))
 
         sums = jnp.sum(squares[...], axis=1, keepdims=True)
         note[stage, 0] = jnp.broadcast_to(sums, (rows, HD)).T[0:8, :]
-        note_copy(stage, 0).start()
+        if stage >= BLOCKS:
+            note_copy(stage, 0).start()
+
+    def send_piece(stage, r):
+        partner_copy(stage, r).start()
+
+        @pl.when(straight)
+        def _():
+            sibling_copy(stage, 1, r).start()
+
+        @pl.when(crossed)
+        def _():
+            other_copy(stage, 0, r).start()
 
     def pass_on(stage):
         @traveling(stage)
@@ -338,14 +340,32 @@
             def _(h):
                 hop_copy(block, h).wait_send()
 
-    send_pieces(0)
+    gain_copy.wait()
+    for block in range(BLOCKS):
+        a_copy(block).wait()
+        make_pieces(block)
+
+    pl.semaphore_wait(
+        barrier, 3 + jnp.where(crossed, 1, 0) + jnp.where(first, 0, 1) + jnp.where(last & (s < sections - 1), 1, 0)
+    )
+
+    @pl.when(jnp.logical_not(first))
+    def _():
+        pl.semaphore_signal(ready, inc=1, device_id=before, device_id_type=MESH)
+
+    for block in range(BLOCKS):
+
+        @pl.loop(0, PIECES)
+        def _(r):
+            send_piece(block, r)
+
+        note_copy(block, 0).start()
 
     @pl.loop(0, heads)
     def _(g):
         for j in range(3):
             w_copy(g, j).start()
 
-    send_pieces(1)
     pass_on(0)
 
     other_sequence(0)
@@ -377,26 +397,28 @@
         def _(g):
             if feeds:
 
-                @pl.when(g == heads - AHEAD)
+                @pl.when(g == SEND_AT)
+                def _():
+                    make_pieces(stage + 1)
+
+                @pl.when(g == PASS_AT)
                 def _():
                     pass_on(stage + 1)
                     other_sequence(stage + 1)
 
-            coming = g + AHEAD
-            if stage < stages - 1:
-                send_part(stage + coming // heads, lax.rem(coming, heads))
-            else:
-
-                @pl.when(coming < heads)
-                def _():
-                    send_part(stage, coming)
-
-            @pl.when(g == DRAIN_AT)
+            @pl.when(g == PASS_AT - 1)
             def _():
                 sent(stage)
                 if layer > 0:
                     hops_sent(block)
 
+            coming = jnp.where(g < PASS_AT, g + AHEAD, g - PASS_AT + heads)
+            ours = coming < heads
+
+            @pl.when(ours if stage == stages - 1 else ours | (g >= PASS_AT))
+            def _():
+                send_part(stage + coming // heads, lax.rem(coming, heads))
+
             here = (tokens(block), head_columns(g))
             result = attend(stage, g)
             if layer == 0:
@@ -412,11 +434,9 @@
             for i in range(2):
                 part_copy(stage, g, i).wait_send()
 
-            if feeds:
-
-                @pl.when(g == SEND_AT)
-                def _():
-                    send_pieces(stage + 1)
+        if stage < stages - 1:
+            for g in range(heads - PASS_AT, AHEAD):
+                send_part(stage + 1, g)
 
 
 def local(sections, inputs, qkv_weight, norm_gain, preempted):
@@ -449,7 +469,7 @@
             pltpu.VMEM((stages, 2, 8, short), f32),
             pltpu.VMEM((stages, 2, 8, short), f32),
             dma((heads, 3)),
-            dma((2,)),
+            dma((BLOCKS + 1,)),
             dma((stages, 2, PIECES)),
             dma((stages, 2, PIECES)),
             dma((stages, PIECES)),

time: 88.2 us -> 87.5 us (level)
  no operation moved by 1% of the time
where the time goes in v4:
time: 87.5 us; the launch traced here: 87.4 us
  Pallas kernels  86 us (98%)
    pallas_call x1, Pallas kernels, local(): pl.pallas_call(functools.partial(kernel, sections, heads), out_shape=jax....  86 us

profile of v4, /device:TPU:24, one launch (start us, length us, event | category | flops | bytes accessed | tf_op | source)
XLA Modules:
  0.0 87.4 jit_solution(12271861149782239087)
XLA Ops:
  0.7 86.0 %relay.1 = bf16[256,896]{1,0:T(8,128)(2,1)S(1)} custom-call(bf16[256,896]{1,0:T(8,128)(2,1)} %bitcast.5, bf16[3,1792,896]{2,1,0:T(8,128)(2,1)} %bitcast.4, bf16[1,3584]{1,0:T(2,128)(2,1)} %gain_hbm.1, s32[1]{0:T(128)S(6)} %copy.6.pre_ref), custom_call_target="tpu_custom_call" | custom-call | flops 9865003008 | bytes 9633792 | tf_op jit(solution)/shard_map/relay/pallas_call | solution.py:451
  86.6 0.8 copy.7

commit v5 on v4

--- a/solution.py
+++ b/solution.py
@@ -11,8 +11,8 @@
 HD = 128
 BLOCKS = 2
 PIECES = 1
-AHEAD = 4
-SEND_AT = 1
+AHEAD = 5
+SEND_AT = 0
 PASS_AT = 4
 COLUMN = 8
 MESH = pl.DeviceIdType.MESH
@@ -29,7 +29,9 @@
     w,
     feats,
     psend,
+    vsend,
     precv,
+    vrecv,
     a_own,
     x_prev,
     own,
@@ -122,9 +124,9 @@
         return remote(there, there, s_send.at[stage, slot, h], s_recv.at[stage, slot, h], sibling)
 
     def part_copy(stage, g, i):
-        here = (stage, g, slice(None), (pl.ds(0, 2 * HD), pl.ds(2 * HD, HD))[i])
         return remote(
-            psend.at[here], precv.at[here], part_send.at[i, stage, g], part_recv.at[i, stage, g], partner
+            (psend, vsend)[i].at[stage, g], (precv, vrecv)[i].at[stage, g],
+            part_send.at[i, stage, g], part_recv.at[i, stage, g], partner,
         )
 
     def hop_copy(block, h):
@@ -286,7 +288,8 @@
 
     def send_part(stage, g):
         part = project(stage, 0, g)
-        psend[stage, g] = part.astype(jnp.bfloat16)
+        psend[stage, g] = part[:, : 2 * HD].astype(jnp.bfloat16)
+        vsend[stage, g] = part[:, 2 * HD :].astype(jnp.bfloat16)
         for i in range(2):
             part_copy(stage, g, i).start()
 
@@ -310,7 +313,7 @@
         powers = jnp.exp(scores - jnp.max(scores, axis=1, keepdims=True))
         chance = (powers * (1.0 / jnp.sum(powers, axis=1, keepdims=True))).astype(jnp.bfloat16)
         part_copy(stage, g, 1).wait_recv()
-        value = (part[:, 2 * HD :] + precv[stage, g, :, 2 * HD :].astype(jnp.float32)) * inverse
+        value = (part[:, 2 * HD :] + vrecv[stage, g].astype(jnp.float32)) * inverse
         values[g, tokens(block)] = value.astype(jnp.bfloat16)
         mixture = jnp.dot(chance, values[g, 0:seen], preferred_element_type=jnp.float32)
         return (layer_input(stage, (tokens(block), head_columns(g))) + mixture).astype(jnp.bfloat16)
@@ -341,9 +344,8 @@
                 hop_copy(block, h).wait_send()
 
     gain_copy.wait()
-    for block in range(BLOCKS):
-        a_copy(block).wait()
-        make_pieces(block)
+    a_copy(0).wait()
+    make_pieces(0)
 
     pl.semaphore_wait(
         barrier, 3 + jnp.where(crossed, 1, 0) + jnp.where(first, 0, 1) + jnp.where(last & (s < sections - 1), 1, 0)
@@ -354,6 +356,9 @@
         pl.semaphore_signal(ready, inc=1, device_id=before, device_id_type=MESH)
 
     for block in range(BLOCKS):
+        if block > 0:
+            a_copy(block).wait()
+            make_pieces(block)
 
         @pl.loop(0, PIECES)
         def _(r):
@@ -456,8 +461,10 @@
         scratch_shapes=[
             pltpu.VMEM((heads, depth, 3 * HD), bf16),
             pltpu.VMEM((stages, 4, 2, short, width), bf16),
-            pltpu.VMEM((stages, heads, short, 3 * HD), bf16),
-            pltpu.VMEM((stages, heads, short, 3 * HD), bf16),
+            pltpu.VMEM((stages, heads, short, 2 * HD), bf16),
+            pltpu.VMEM((stages, heads, short, HD), bf16),
+            pltpu.VMEM((stages, heads, short, 2 * HD), bf16),
+            pltpu.VMEM((stages, heads, short, HD), bf16),
             pltpu.VMEM((rows, width), bf16),
             pltpu.VMEM((rows, width), bf16),
             pltpu.VMEM((rows, width), bf16),

time: 87.5 us -> 87 us (level)
  no operation moved by 1% of the time
where the time goes in v5:
time: 87 us; the launch traced here: 86.8 us
  Pallas kernels  85.4 us (98%)
    pallas_call x1, Pallas kernels, local(): pl.pallas_call(functools.partial(kernel, sections, heads), out_shape=jax....  85.4 us

profile of v5, /device:TPU:24, one launch (start us, length us, event | category | flops | bytes accessed | tf_op | source)
XLA Modules:
  0.0 86.8 jit_solution(9088984953854011068)
XLA Ops:
  0.7 85.4 %relay.1 = bf16[256,896]{1,0:T(8,128)(2,1)S(1)} custom-call(bf16[256,896]{1,0:T(8,128)(2,1)} %bitcast.5, bf16[3,1792,896]{2,1,0:T(8,128)(2,1)} %bitcast.4, bf16[1,3584]{1,0:T(2,128)(2,1)} %gain_hbm.1, s32[1]{0:T(128)S(6)} %copy.6.pre_ref), custom_call_target="tpu_custom_call" | custom-call | flops 9865003008 | bytes 9633792 | tf_op jit(solution)/shard_map/relay/pallas_call | solution.py:456
  86.0 0.8 copy.7
